TPU v7x, 32 devices: a whole 2x2x4 slice. The times are simulated.
32 devices in a mesh: groups: 2 (over y), dom: 4 (over z), feat: 2 (over x), sub: 2 (over core).
Axes of the slice: x: 2, y: 2, z: 4, core: 2. Of those that a mesh axis runs over, the one named last changes fastest.
Arguments:
- grid_lat: bfloat16 [16384, 512], P(('groups', 'dom', 'feat', 'sub')), parts along dimension 0, may hold values from -6 to 6
- mesh_lat: bfloat16 [8192, 512], P(('groups', 'dom', 'feat', 'sub')), parts along dimension 0, may hold values from -6 to 6
- g2m_src: int32 [32, 64], P(('groups', 'dom', 'feat', 'sub')), parts along dimension 0, may hold values from 0 to 511
- g2m_dst: int32 [32, 64], P(('groups', 'dom', 'feat', 'sub')), parts along dimension 0, may hold values from 0 to 511
- g2m_count: int32 [32, 8], P(('groups', 'dom', 'feat', 'sub')), parts along dimension 0, may hold values from 0 to 8, as said below
- g2m_dist: bfloat16 [32, 64], P(('groups', 'dom', 'feat', 'sub')), parts along dimension 0, may hold values from 0.5 to 1.5
- m2m_src: int32 [32, 1536], P(('groups', 'dom', 'feat', 'sub')), parts along dimension 0, may hold values from 0 to 767
- m2m_dst: int32 [32, 1536], P(('groups', 'dom', 'feat', 'sub')), parts along dimension 0, may hold values from 0 to 511
- m2m_count: int32 [32, 1], P(('groups', 'dom', 'feat', 'sub')), parts along dimension 0, may hold values from 512 to 1536, as said below
- m2m_dist: float32 [32, 1536], P(('groups', 'dom', 'feat', 'sub')), parts along dimension 0, may hold values from 0.5 to 1.5
- enc_edge: bfloat16 [2, 512, 512], replicated, may hold values from -0.25 to 0.25
- enc_node_in: bfloat16 [2, 512, 512], replicated, may hold values from -0.25 to 0.25
- enc_node_out: bfloat16 [512, 512], replicated, may hold values from -0.25 to 0.25
- proc_edge: bfloat16 [2, 512, 512], replicated, may hold values from -0.25 to 0.25
- enc_vecs: float32 [3, 512], replicated, may hold values from -3 to 3
- proc_vecs: float32 [2, 512], replicated, may hold values from -3 to 3
Outputs:
- mesh_enc: bfloat16 [8192, 512], P(('groups', 'dom', 'feat', 'sub')), parts along dimension 0
- mesh_agg: bfloat16 [8192, 512], P(('groups', 'dom', 'feat', 'sub')), parts along dimension 0
There are 2 independent parts, one for each index of `groups`. A program takes and returns all parts, laid end to end along the dimension named above; an argument that names none is the same for every part. Nothing has to cross between parts.
Inputs may be any that keep to these rules, and one draw needn't show every extreme that they name: `g2m_count`: in every draw one owner receives 8 live slots from every sender. `m2m_count`: live slots stand at the head of each block; one device's block is full in every draw.
All inputs are finite; a program needn't handle non-finite values.
Results may differ from a plain program's by a relative error of at most 0.0058.
Values may be sent and summed in bfloat16 or wider, within the bound.
A program may use at most 64 MiB of HBM per device.

v0:
```python
import jax
import jax.numpy as jnp
from jax import lax
from jax.sharding import PartitionSpec as P

CAP = 8
RIM = 128


def extended_2(value, sides, width):
    for axis, dim in sides:
        size, length = (lax.axis_size(axis), value.shape[dim])
        up = [(i, (i + 1) % size) for i in range(size - 1)]
        down = [(j, i) for i, j in up]
        last = lax.slice_in_dim(value, length - width, length, axis=dim)
        initial = lax.slice_in_dim(value, 0, width, axis=dim)
        before = lax.ppermute(last, axis, up)
        after = lax.ppermute(initial, axis, down)
        value = jnp.concatenate([before, value, after], axis=dim)
    return value


def owner_block(shard):
    return lax.all_gather(shard, "sub", axis=0, tiled=True)


def edge_aggregate(source_terms, receiver_proj, edge_tags, edge_lengths, section_vectors):
    receiver = jnp.where(edge_tags >= 0, edge_tags, 0)
    pre_act = source_terms + jnp.take(receiver_proj, receiver, axis=0)
    pre_act = (
        pre_act
        + edge_lengths.astype(jnp.float32)[:, None] * section_vectors[1]
        + section_vectors[0]
    )
    hidden_edge = jax.nn.silu(pre_act).astype(jnp.bfloat16)
    node_ids = jnp.arange(receiver_proj.shape[0], dtype=jnp.int32)
    incidence = (node_ids[:, None] == edge_tags[None, :]).astype(jnp.bfloat16)
    partial_value = jnp.dot(incidence, hidden_edge, preferred_element_type=jnp.float32)
    return lax.psum_scatter(
        partial_value.astype(jnp.bfloat16), "sub", scatter_dimension=0, tiled=True
    )


def node_update(own_rows, aggregate, weight_first, weight_second, weight_out, bias_row):
    pre_act = jnp.dot(own_rows, weight_first, preferred_element_type=jnp.float32)
    pre_act = (
        pre_act + jnp.dot(aggregate, weight_second, preferred_element_type=jnp.float32) + bias_row
    )
    hidden_node = jax.nn.silu(pre_act).astype(jnp.bfloat16)
    update = jnp.dot(hidden_node, weight_out, preferred_element_type=jnp.float32)
    return (own_rows.astype(jnp.float32) + update).astype(jnp.bfloat16)


def on_device(
    grid_lat,
    mesh_lat,
    g2m_src,
    g2m_dst,
    g2m_count,
    g2m_dist,
    m2m_src,
    m2m_dst,
    m2m_count,
    m2m_dist,
    enc_edge,
    enc_node_in,
    enc_node_out,
    proc_edge,
    enc_vecs,
    proc_vecs,
):
    owner_rows = owner_block(mesh_lat)
    grid_proj = jnp.dot(grid_lat, enc_edge[0], preferred_element_type=jnp.float32).astype(
        jnp.bfloat16
    )
    receiver_proj = jnp.dot(owner_rows, enc_edge[1], preferred_element_type=jnp.float32)
    live_slots = (jnp.arange(CAP, dtype=jnp.int32)[None, :] < g2m_count[0][:, None]).reshape(-1)
    slot_tags = jnp.where(live_slots, g2m_dst[0], -1)
    slot_rows = jnp.take(grid_proj, g2m_src[0], axis=0)
    slot_lengths = g2m_dist[0]
    got_rows, got_lengths, got_tags = (
        lax.all_to_all(slot_rows, ("dom", "feat"), split_axis=0, concat_axis=0, tiled=True),
        lax.all_to_all(slot_lengths, ("dom", "feat"), split_axis=0, concat_axis=0, tiled=True),
        lax.all_to_all(slot_tags, ("dom", "feat"), split_axis=0, concat_axis=0, tiled=True),
    )
    aggregate = edge_aggregate(
        got_rows.astype(jnp.float32), receiver_proj, got_tags, got_lengths, enc_vecs
    )
    mesh_enc = node_update(
        mesh_lat, aggregate, enc_node_in[0], enc_node_in[1], enc_node_out, enc_vecs[2]
    )
    edge_live = jnp.arange(m2m_src.shape[1], dtype=jnp.int32) < m2m_count[0, 0]
    edge_tags = jnp.where(edge_live, m2m_dst[0], -1)
    owner_rows = owner_block(mesh_enc)
    extended = extended_2(owner_rows, ((("dom", "feat"), 0),), RIM)
    source_proj = jnp.dot(extended, proc_edge[0], preferred_element_type=jnp.float32)
    receiver_proj = jnp.dot(owner_rows, proc_edge[1], preferred_element_type=jnp.float32)
    source_terms = jnp.take(source_proj, m2m_src[0], axis=0)
    mesh_agg = edge_aggregate(source_terms, receiver_proj, edge_tags, m2m_dist[0], proc_vecs)
    return (mesh_enc, mesh_agg)


def solution(mesh):
    in_specs = (
        P(("groups", "dom", "feat", "sub"), None),
        P(("groups", "dom", "feat", "sub"), None),
        P(("groups", "dom", "feat", "sub"), None),
        P(("groups", "dom", "feat", "sub"), None),
        P(("groups", "dom", "feat", "sub"), None),
        P(("groups", "dom", "feat", "sub"), None),
        P(("groups", "dom", "feat", "sub"), None),
        P(("groups", "dom", "feat", "sub"), None),
        P(("groups", "dom", "feat", "sub"), None),
        P(("groups", "dom", "feat", "sub"), None),
        P(),
        P(),
        P(),
        P(),
        P(),
        P(),
    )
    out_specs = (
        P(("groups", "dom", "feat", "sub"), None),
        P(("groups", "dom", "feat", "sub"), None),
    )
    return jax.shard_map(
        on_device, mesh=mesh, in_specs=in_specs, out_specs=out_specs, check_vma=False
    )
```

profile of v0, /device:TPU:0, one launch (start us, length us, event | category | flops | bytes accessed | tf_op | source)
XLA Modules:
  0.0 102.6 jit_solution(6451524131043851978)
XLA Ops:
  7.2 0.0 copy-start
  7.2 0.5 broadcast.243
  7.7 1.3 %reduce.30 = bf16[64]{0:T(256)(128)(2,1)S(1)} reduce(bf16[1,64]{1,0:T(2,128)(2,1)} %param.21, bf16[]{:T(256)} %broadcast.243), dimensions={0}, to_apply=%param.21.reduce_sub_computation.3 | reduce | bytes 258 | tf_op args[5]
  9.0 0.7 all_to_all.21
  9.7 7.3 %all-to-all-start.2 = ((bf16[8,8,1]{1,2,0:T(2,128)(2,1)}), bf16[8,8,1]{1,2,0:T(2,128)(2,1)S(1)}, u32[]{:S(2)}, u32[]{:S(2)}) async-start(bf16[8,8,1]{1,2,0:T(2,128)(2,1)} %all_to_all.21), calls=%async_computation.2 | async-start | bytes 8192 | tf_op jit(solution)/shard_map/all_to_all | solution.py:83
  17.0 0.7 fusion.47
  17.6 0.5 broadcast.240
  18.1 1.2 %reduce.29 = s32[64]{0:T(128)S(1)} reduce(s32[1,64]{1,0:T(1,128)} %param.18, s32[]{:T(128)} %broadcast.240), dimensions={0}, to_apply=%param.18.reduce_sub_computation.3 | reduce | bytes 516 | tf_op args[2]
  19.4 1.2 %reduce.27 = s32[64]{0:T(128)S(1)} reduce(s32[1,64]{1,0:T(1,128)} %param.19, s32[]{:T(128)} %broadcast.240), dimensions={0}, to_apply=%param.19.reduce_sub_computation.3 | reduce | bytes 516 | tf_op args[3]
  20.6 0.1 squeeze.41
  20.7 2.4 %all_gather.6 = bf16[512,512]{1,0:T(8,128)(2,1)S(1)} all-gather(bf16[256,512]{1,0:T(8,128)(2,1)} %param.17), channel_id=1, replica_groups=mesh['groups'=2,'dom'=4,'feat'=2,'sub'=2] {'sub'}, dimensions={0}, use_global_device_ids=true | all-gather | bytes 786432 | tf_op jit(solution)/shard_map/all_gather | solution.py:24
  23.1 0.1 squeeze.42
  23.2 1.5 %fusion.15 = f32[512,512]{1,0:T(8,128)S(1)} fusion(bf16[512,512]{1,0:T(8,128)(2,1)S(1)} %all_gather.6, bf16[2,512,512]{2,1,0:T(8,128)(2,1)} %param.26), kind=kOutput, calls=%fused_computation.25 | convolution fusion | flops 268435456 | bytes 2097152 | tf_op jit(solution)/shard_map/dot_general | solution.py:76
  24.7 0.0 copy-start.6
  24.7 0.0 copy-start.5
  24.7 0.0 copy-start.8
  24.7 0.0 copy-start.1
  24.7 0.0 copy-start.3
  24.7 1.6 %convolution_convert_fusion = bf16[512,512]{1,0:T(8,128)(2,1)S(1)} fusion(bf16[512,512]{1,0:T(8,128)(2,1)S(1)} %copy-done, bf16[2,512,512]{2,1,0:T(8,128)(2,1)} %param.26), kind=kOutput, calls=%fused_computation.9 | convolution fusion | flops 268697600 | bytes 1572864 | tf_op jit(solution)/shard_map/dot_general | solution.py:73
  26.3 0.7 fusion.46
  27.0 0.7 gather_fusion
  27.7 0.7 bitcast_select_fusion
  28.5 6.0 %all-to-all-start = ((s32[8,8,1]{1,2,0:T(1,128)}), s32[8,8,1]{1,2,0:T(1,128)S(1)}, u32[]{:S(2)}, u32[]{:S(2)}) async-start(s32[8,8,1]{1,2,0:T(1,128)} %bitcast.2), calls=%async_computation | async-start | bytes 8192 | tf_op jit(solution)/shard_map/all_to_all | solution.py:84
  34.5 0.1 reshape.226
  34.6 6.3 %all-to-all-done = s32[8,8,1]{1,2,0:T(1,128)S(1)} async-done(((s32[8,8,1]{1,2,0:T(1,128)}), s32[8,8,1]{1,2,0:T(1,128)S(1)}, u32[]{:S(2)}, u32[]{:S(2)}) %all-to-all-start) | async-done | bytes 288 | tf_op jit(solution)/shard_map/all_to_all | solution.py:84
  40.9 3.4 %all-to-all-start.1 = ((bf16[8,8,512]{2,1,0:T(8,128)(2,1)}), bf16[8,8,512]{2,1,0:T(8,128)(2,1)S(1)}, u32[]{:S(2)}, u32[]{:S(2)}) async-start(bf16[8,8,512]{2,1,0:T(8,128)(2,1)} %bitcast_select_fusion), calls=%async_computation.1 | async-start | bytes 131072 | tf_op jit(solution)/shard_map/all_to_all | solution.py:82
  44.2 0.0 reduce-scatter.3.cloned.1.call-start
  44.3 0.6 reduce.28
  44.9 0.1 eq.31
  44.9 0.1 all_to_all.18
  45.0 0.7 gather_fusion.1
  45.7 5.4 %all-to-all-done.1 = bf16[8,8,512]{2,1,0:T(8,128)(2,1)S(1)} async-done(((bf16[8,8,512]{2,1,0:T(8,128)(2,1)}), bf16[8,8,512]{2,1,0:T(8,128)(2,1)S(1)}, u32[]{:S(2)}, u32[]{:S(2)}) %all-to-all-start.1) | async-done | bytes 65568 | tf_op jit(solution)/shard_map/all_to_all | solution.py:82
  51.1 1.2 %convolution_convert_fusion.1 = bf16[512,512]{1,0:T(8,128)(2,1)} fusion(s32[64]{0:T(128)S(1)} %eq.31, f32[64,512]{1,0:T(8,128)S(1)} %gather_fusion.1, bf16[8,8,512]{2,1,0:T(8,128)(2,1)S(1)} %all-to-all-done.1, f32[512]{0:T(512)S(1)} %bitcast.64, f32[512]{0:T(512)S(1)} %bitcast.63, f32[64]{0:T(128)S(1)} %reshape.226, pred[64]{0:T(512)(128)(4,1)S(1)} %compare_and_fusion.3), kind=kOutput, calls=%fused_computation.10 | convolution fusion | flops 34209792 | bytes 725568 | tf_op jit(solution)/shard_map/dot_general | solution.py:38
  52.3 0.0 reduce-scatter.3.cloned.1.call-update
  52.3 0.0 reduce-scatter.5.cloned.1.call-start
  53.2 0.3 fusion.18
  53.5 4.4 %reduce-scatter.3.cloned.1.call-done = bf16[256,512]{1,0:T(8,128)(2,1)} async-done(((bf16[512,512]{1,0:T(8,128)(2,1)}), bf16[256,512]{1,0:T(8,128)(2,1)}) %reduce-scatter.3.cloned.1.call-update) | async-done | bytes 262160 | tf_op jit(solution)/shard_map/reduce_scatter | solution.py:39
  57.9 1.7 %fusion.4 = bf16[256,512]{1,0:T(8,128)(2,1)S(1)} fusion(bf16[512,512]{1,0:T(8,128)(2,1)} %param.28, f32[256,512]{1,0:T(8,128)S(1)} %fusion.18, bf16[256,512]{1,0:T(8,128)(2,1)} %reduce-scatter.3.cloned.1.call-done, bf16[2,512,512]{2,1,0:T(8,128)(2,1)S(1)} %copy-done.3, bf16[256,512]{1,0:T(8,128)(2,1)S(1)} %copy-done.1, f32[512]{0:T(512)S(1)} %bitcast.62), kind=kOutput, calls=%fused_computation.14 | convolution fusion | flops 269746176 | bytes 2361344 | tf_op jit(solution)/shard_map/dot_general | solution.py:50
  59.6 2.2 %all_gather.7 = bf16[512,512]{1,0:T(8,128)(2,1)S(1)} all-gather(bf16[256,512]{1,0:T(8,128)(2,1)S(1)} %fusion.4), channel_id=1, replica_groups=mesh['groups'=2,'dom'=4,'feat'=2,'sub'=2] {'sub'}, dimensions={0}, use_global_device_ids=true | all-gather | bytes 786432 | tf_op jit(solution)/shard_map/all_gather | solution.py:24
  61.8 3.6 %collective-permute-start = (bf16[128,512]{1,0:T(8,128)(2,1)S(1)}, bf16[128,512]{1,0:T(8,128)(2,1)S(1)}, u32[]{:S(2)}, u32[]{:S(2)}) collective-permute-start(bf16[128,512]{1,0:T(8,128)(2,1)S(1)} %get-tuple-element.4), channel_id=1, source_target_pairs={{0,2},{2,4},{4,6},{6,8},{8,10},{10,12},{12,14},{1,3},{3,5},{5,7},{... | collective-permute-start | bytes 393224 | tf_op jit(solution)/shard_map/ppermute | solution.py:17
  65.5 1.3 %collective-permute-start.1 = (bf16[128,512]{1,0:T(8,128)(2,1)S(1)}, bf16[128,512]{1,0:T(8,128)(2,1)S(1)}, u32[]{:S(2)}, u32[]{:S(2)}) collective-permute-start(bf16[128,512]{1,0:T(8,128)(2,1)S(1)} %get-tuple-element.5), channel_id=1, source_target_pairs={{2,0},{4,2},{6,4},{8,6},{10,8},{12,10},{14,12},{3,1},{5,3},{7,5},{... | collective-permute-start | bytes 393224 | tf_op jit(solution)/shard_map/ppermute | solution.py:18
  66.8 1.5 %fusion.11 = f32[512,512]{1,0:T(8,128)S(1)} fusion(bf16[512,512]{1,0:T(8,128)(2,1)S(1)} %all_gather.7, bf16[2,512,512]{2,1,0:T(8,128)(2,1)} %param.29), kind=kOutput, calls=%fused_computation.21 | convolution fusion | flops 268435456 | bytes 2097152 | tf_op jit(solution)/shard_map/dot_general | solution.py:97
  68.2 5.0 %gather_fusion.3 = f32[1536,512]{1,0:T(8,128)} fusion(f32[512,512]{1,0:T(8,128)S(1)} %fusion.11, s32[2048]{0:T(1024)S(1)} %pad_clamp_fusion), kind=kCustom, calls=%fused_computation.3 | custom fusion | bytes 6297600 | tf_op jit(solution)/shard_map/jit(_take)/gather | solution.py:29
  73.2 1.6 %fusion.5 = f32[768,512]{1,0:T(8,128)S(1)} fusion(bf16[128,512]{1,0:T(8,128)(2,1)S(1)} %collective-permute-done.1, bf16[512,512]{1,0:T(8,128)(2,1)S(1)} %all_gather.7, bf16[128,512]{1,0:T(8,128)(2,1)S(1)} %collective-permute-done, bf16[2,512,512]{2,1,0:T(8,128)(2,1)} %param.29), kind=kOutput, calls=%fused_computation.15 | convolution fusion | flops 405012480 | bytes 2883584 | tf_op jit(solution)/shard_map/dot_general | solution.py:96
  74.8 5.0 %gather_fusion.2 = f32[1536,512]{1,0:T(8,128)} fusion(f32[768,512]{1,0:T(8,128)S(1)} %fusion.5, s32[2048]{0:T(1024)S(1)} %pad_clamp_fusion.1), kind=kCustom, calls=%fused_computation.2 | custom fusion | bytes 6297600 | tf_op jit(solution)/shard_map/jit(_take)/gather | solution.py:98
  79.8 5.7 %fusion.2 = bf16[512,512]{1,0:T(8,128)(2,1)} fusion(f32[1536,512]{1,0:T(8,128)} %gather_fusion.3, f32[1536,512]{1,0:T(8,128)} %gather_fusion.2, f32[512]{0:T(512)S(1)} %bitcast.66, f32[512]{0:T(512)S(1)} %bitcast.65, f32[1536]{0:T(1024)S(1)} %reduce.11, pred[1536]{0:T(1024)(128)(4,1)S(1)} %get-tuple-element.11, pred[1536]{0:T(1024)(128)(4,1)S(1)} %get-tuple-element.12, ...), kind=kOutput, calls=%fused_computation.8 | convolution fusion | flops 815005696 | bytes 6835200 | tf_op jit(solution)/shard_map/dot_general | solution.py:38
  85.5 0.0 reduce-scatter.5.cloned.1.call-update
  85.5 10.2 %reduce-scatter.5.cloned.1.call-done = bf16[256,512]{1,0:T(8,128)(2,1)} async-done(((bf16[512,512]{1,0:T(8,128)(2,1)}), bf16[256,512]{1,0:T(8,128)(2,1)}) %reduce-scatter.5.cloned.1.call-update) | async-done | bytes 262160 | tf_op jit(solution)/shard_map/reduce_scatter | solution.py:39
  (34 shorter events, 0.3 us)
Async XLA Ops:
  7.2 17.5 %copy-start = (bf16[512,512]{1,0:T(8,128)(2,1)S(1)}, bf16[512,512]{1,0:T(8,128)(2,1)}, u32[]{:S(2)}) copy-start(bf16[512,512]{1,0:T(8,128)(2,1)} %param.16) | copy-start | bytes 1572868
  7.2 19.1 %copy-start.7 = (f32[3,512]{1,0:T(4,128)S(1)}, f32[3,512]{1,0:T(4,128)}, u32[]{:S(2)}) copy-start(f32[3,512]{1,0:T(4,128)} %param.30) | copy-start | bytes 18436
  7.2 19.2 %copy-start.9 = (s32[1,8]{1,0:T(1,128)S(1)}, s32[1,8]{1,0:T(1,128)}, u32[]{:S(2)}) copy-start(s32[1,8]{1,0:T(1,128)} %param.20) | copy-start | bytes 100
  7.2 21.2 %copy-start.4 = (s32[1,1536]{1,0:T(1,128)S(1)}, s32[1,1536]{1,0:T(1,128)}, u32[]{:S(2)}) copy-start(s32[1,1536]{1,0:T(1,128)} %param.22) | copy-start | bytes 18436
  9.7 18.7 %all-to-all-start.2 = ((bf16[8,8,1]{1,2,0:T(2,128)(2,1)}), bf16[8,8,1]{1,2,0:T(2,128)(2,1)S(1)}, u32[]{:S(2)}, u32[]{:S(2)}) async-start(bf16[8,8,1]{1,2,0:T(2,128)(2,1)} %all_to_all.21), calls=%async_computation.2 | async-start | bytes 8192 | tf_op jit(solution)/shard_map/all_to_all | solution.py:83
  24.7 28.4 %copy-start.6 = (f32[1,1536]{1,0:T(1,128)S(1)}, f32[1,1536]{1,0:T(1,128)}, u32[]{:S(2)}) copy-start(f32[1,1536]{1,0:T(1,128)} %param.25) | copy-start | bytes 18436
  24.7 28.4 %copy-start.5 = (s32[1,1536]{1,0:T(1,128)S(1)}, s32[1,1536]{1,0:T(1,128)}, u32[]{:S(2)}) copy-start(s32[1,1536]{1,0:T(1,128)} %param.23) | copy-start | bytes 18436
  24.7 28.5 %copy-start.8 = (f32[2,512]{1,0:T(2,128)S(1)}, f32[2,512]{1,0:T(2,128)}, u32[]{:S(2)}) copy-start(f32[2,512]{1,0:T(2,128)} %param.31) | copy-start | bytes 12292
  24.7 28.5 %copy-start.1 = (bf16[256,512]{1,0:T(8,128)(2,1)S(1)}, bf16[256,512]{1,0:T(8,128)(2,1)}, u32[]{:S(2)}) copy-start(bf16[256,512]{1,0:T(8,128)(2,1)} %param.17) | copy-start | bytes 786436
  24.7 28.5 %copy-start.3 = (bf16[2,512,512]{2,1,0:T(8,128)(2,1)S(1)}, bf16[2,512,512]{2,1,0:T(8,128)(2,1)}, u32[]{:S(2)}) copy-start(bf16[2,512,512]{2,1,0:T(8,128)(2,1)} %param.27) | copy-start | bytes 3145732
  28.5 12.4 %all-to-all-start = ((s32[8,8,1]{1,2,0:T(1,128)}), s32[8,8,1]{1,2,0:T(1,128)S(1)}, u32[]{:S(2)}, u32[]{:S(2)}) async-start(s32[8,8,1]{1,2,0:T(1,128)} %bitcast.2), calls=%async_computation | async-start | bytes 8192 | tf_op jit(solution)/shard_map/all_to_all | solution.py:84
  40.9 10.2 %all-to-all-start.1 = ((bf16[8,8,512]{2,1,0:T(8,128)(2,1)}), bf16[8,8,512]{2,1,0:T(8,128)(2,1)S(1)}, u32[]{:S(2)}, u32[]{:S(2)}) async-start(bf16[8,8,512]{2,1,0:T(8,128)(2,1)} %bitcast_select_fusion), calls=%async_computation.1 | async-start | bytes 131072 | tf_op jit(solution)/shard_map/all_to_all | solution.py:82
  44.2 13.7 %reduce-scatter.3.cloned.1.call-start = ((), (), s32[]{:S(2)}) async-start(), calls=%async_computation.5 | async-start | bytes 786432 | tf_op jit(solution)/shard_map/reduce_scatter | solution.py:39
  52.3 43.4 %reduce-scatter.5.cloned.1.call-start = ((), (), s32[]{:S(2)}) async-start(), calls=%async_computation.6 | async-start | bytes 786432 | tf_op jit(solution)/shard_map/reduce_scatter | solution.py:39
  59.6 13.6 %copy-start.2 = (bf16[256,512]{1,0:T(8,128)(2,1)}, bf16[256,512]{1,0:T(8,128)(2,1)S(1)}, u32[]{:S(2)}) copy-start(bf16[256,512]{1,0:T(8,128)(2,1)S(1)} %fusion.4) | copy-start | bytes 786436
  61.8 11.4 %collective-permute-start = (bf16[128,512]{1,0:T(8,128)(2,1)S(1)}, bf16[128,512]{1,0:T(8,128)(2,1)S(1)}, u32[]{:S(2)}, u32[]{:S(2)}) collective-permute-start(bf16[128,512]{1,0:T(8,128)(2,1)S(1)} %get-tuple-element.4), channel_id=1, source_target_pairs={{0,2},{2,4},{4,6},{6,8},{8,10},{10,12},{12,14},{1,3},{3,5},{5,7},{... | collective-permute-start | bytes 393224 | tf_op jit(solution)/shard_map/ppermute | solution.py:17
  65.5 7.7 %collective-permute-start.1 = (bf16[128,512]{1,0:T(8,128)(2,1)S(1)}, bf16[128,512]{1,0:T(8,128)(2,1)S(1)}, u32[]{:S(2)}, u32[]{:S(2)}) collective-permute-start(bf16[128,512]{1,0:T(8,128)(2,1)S(1)} %get-tuple-element.5), channel_id=1, source_target_pairs={{2,0},{4,2},{6,4},{8,6},{10,8},{12,10},{14,12},{3,1},{5,3},{7,5},{... | collective-permute-start | bytes 393224 | tf_op jit(solution)/shard_map/ppermute | solution.py:18
Sparse Core Ops, SparseCore 0:
  52.4 5.4 reduce-scatter.2
  85.6 10.0 reduce-scatter.4
where the time goes:
time: 103 us
  waiting for transfers between devices  26.2 us (25%)
  starting transfers between devices  21.6 us (21%)
  matrix products  15.1 us (15%)
  between operations  15 us (15%)
  local copies, waits for them, and re-layouts  13.4 us (13%)
  other arithmetic  6.61 us (6%)
  blocking collectives  4.57 us (4%)
    reduce_scatter x2, waiting for transfers between devices, edge_aggregate(): lax.psum_scatter(partial_value.astype(jnp.bfloat16), 'sub', scatter_dimen...  14.6 us
    all_to_all x1, starting transfers between devices, on_device(): lax.all_to_all(slot_lengths, ('dom', 'feat'), split_axis=0, concat_axis=0...  7.25 us
    dot_general x2, matrix products, edge_aggregate(): jnp.dot(incidence, hidden_edge, preferred_element_type=jnp.float32)  6.93 us
    all_to_all x1, waiting for transfers between devices, on_device(): lax.all_to_all(slot_tags, ('dom', 'feat'), split_axis=0, concat_axis=0, t...  6.29 us
    all_to_all x1, starting transfers between devices, on_device(): lax.all_to_all(slot_tags, ('dom', 'feat'), split_axis=0, concat_axis=0, t...  6.01 us
    gather x2, local copies, waits for them, and re-layouts, edge_aggregate(): pre_act = source_terms + jnp.take(receiver_proj, receiver, axis=0)  5.61 us
    all_to_all x1, waiting for transfers between devices, on_device(): lax.all_to_all(slot_rows, ('dom', 'feat'), split_axis=0, concat_axis=0, t...  5.36 us
    gather x1, local copies, waits for them, and re-layouts, on_device(): source_terms = jnp.take(source_proj, m2m_src[0], axis=0)  4.95 us
  transfers between devices with their start and end apart: 7, of which 4 were waited for; matrix products, arithmetic and copies ran while one was open for 17% of the time, Pallas kernels for 0%

commit v1 on v0

v1 whole, which is shorter than its diff:
```python
import functools

import jax
import jax.numpy as jnp
from jax import lax
from jax.experimental import pallas as pl
from jax.experimental.pallas import tpu as pltpu
from jax.sharding import PartitionSpec as P

CAP = 8
RIM = 128
LANES = 128
PARTS = 2
MESH = pl.DeviceIdType.MESH
BF16 = jnp.bfloat16
F32 = jnp.float32


def silu(value):
    half = 0.5 * value
    return half + half * jnp.tanh(half)


def dot(left, right):
    return jnp.dot(left, right, preferred_element_type=F32)


def column(row):
    return jnp.transpose(jnp.broadcast_to(row.astype(F32), (LANES, row.shape[1])))


def lane_ids(rows, block):
    ids = lax.broadcasted_iota(jnp.int32, (rows, LANES), 1) + block * LANES
    return ids.astype(F32)


def one_hot(col, width):
    parts = [
        jnp.where(col == lane_ids(col.shape[0], block), 1.0, 0.0)
        for block in range(width // LANES)
    ]
    return jnp.concatenate(parts, axis=1).astype(BF16)


def kernel(
    owners,
    feats,
    grid_hbm,
    mesh_hbm,
    gsrc_ref,
    gdst_ref,
    gcount_ref,
    gdist_ref,
    msrc_ref,
    mdst_ref,
    mcount_ref,
    mdist_ref,
    we_hbm,
    wn_hbm,
    wo_hbm,
    wp_hbm,
    evec_ref,
    pvec_ref,
    enc_out,
    agg_out,
    grid_ref,
    mesh_ref,
    we_ref,
    wn_ref,
    wo_ref,
    wp_ref,
    msg_ref,
    got_ref,
    got2_ref,
    base_ref,
    hot_ref,
    hot_t_ref,
    ext_ref,
    table_ref,
    acc_ref,
    hid_ref,
    part_ref,
    other_ref,
    load_sem,
    a2a_send,
    a2a_recv,
    fwd_send,
    fwd_recv,
    sib_send,
    sib_recv,
    rim_send,
    rim_recv,
    rfw_send,
    rfw_recv,
    par_send,
    par_recv,
):
    sub = lax.axis_index("sub")
    me = lax.axis_index("dom") * feats + lax.axis_index("feat")
    rows, width = mesh_ref.shape
    half = width // 2
    edges = msrc_ref.shape[1]
    own2 = 2 * rows
    sibling = {"sub": 1 - sub}

    def owner_id(owner):
        return {"dom": lax.div(owner, feats), "feat": lax.rem(owner, feats)}

    def send(src, dst, sems, device):
        return pltpu.make_async_remote_copy(
            src_ref=src,
            dst_ref=dst,
            send_sem=sems[0],
            recv_sem=sems[1],
            device_id=device,
            device_id_type=MESH,
        )

    barrier = pltpu.get_barrier_semaphore()
    pl.semaphore_signal(barrier, inc=1, device_id=sibling, device_id_type=MESH)
    for k in range(1, owners):
        pl.semaphore_signal(
            barrier, inc=1, device_id=owner_id(lax.rem(me + k, owners)), device_id_type=MESH
        )

    pairs = (
        (grid_hbm, grid_ref),
        (we_hbm, we_ref),
        (mesh_hbm, mesh_ref),
        (wn_hbm, wn_ref),
        (wo_hbm, wo_ref),
        (wp_hbm, wp_ref),
    )
    loads = [
        pltpu.make_async_copy(src, dst, load_sem.at[i]) for i, (src, dst) in enumerate(pairs)
    ]
    for load in loads:
        load.start()

    gdst = gdst_ref[...]
    upper = (gdst >= rows).astype(jnp.int32)
    upper_col = column(upper)
    lower_col = column(gdst - rows * upper)
    length_col = column(gdist_ref[...])
    source_hot = one_hot(column(gsrc_ref[...]), grid_ref.shape[0])
    slot = lax.broadcasted_iota(jnp.int32, (CAP, LANES), 0)
    live = jnp.concatenate(
        [jnp.where(slot < gcount_ref[0, o], 1.0, 0.0) for o in range(owners)], axis=0
    )
    lower_col = jnp.where(live > 0.5, lower_col, -1.0)
    loads[0].wait()
    picked = dot(source_hot, grid_ref[...]).astype(BF16)
    loads[1].wait()
    term = dot(picked, we_ref[0])
    term = term + jnp.concatenate([length_col] * (width // LANES), axis=1) * evec_ref[1:2, :]
    term = term + evec_ref[0:1, :]
    top = jnp.concatenate([term[:, :half], lower_col], axis=1)
    bottom = jnp.concatenate([term[:, half:], upper_col], axis=1)
    top = top.reshape(owners, CAP, half + LANES)
    bottom = bottom.reshape(owners, CAP, half + LANES)
    msg_ref[...] = jnp.concatenate([top, bottom], axis=1).astype(BF16)

    pl.semaphore_wait(barrier, owners)
    sends = [
        send(
            msg_ref.at[lax.rem(me + k, owners)],
            got_ref.at[k],
            (a2a_send.at[k], a2a_recv.at[k]),
            owner_id(lax.rem(me + k, owners)),
        )
        for k in range(1, owners)
    ]
    for copy in sends:
        copy.start()
    forwards = [
        send(got_ref.at[k], got2_ref.at[k], (fwd_send.at[k], fwd_recv.at[k]), sibling)
        for k in range(owners)
    ]
    got_ref[0] = msg_ref[me]
    forwards[0].start()

    loads[2].wait()
    receiver_proj = dot(mesh_ref[...], we_ref[1]).astype(BF16)
    loads[3].wait()
    base_ref[...] = dot(mesh_ref[...], wn_ref[0]) + evec_ref[2:3, :]
    edge = lax.broadcasted_iota(jnp.int32, (1, edges), 1)
    tags = jnp.where(edge < mcount_ref[0, 0], mdst_ref[...], -1)
    node = lax.broadcasted_iota(jnp.int32, (own2, edges), 0)
    hot_t_ref[...] = jnp.where(node == tags, 1.0, 0.0).astype(BF16)
    source_col = column(msrc_ref[...])
    hot_ref[:, 0:own2] = one_hot(source_col - RIM, own2)
    hot_ref[:, own2 : 2 * own2] = one_hot(column(tags), own2)
    rim_col = jnp.where(source_col >= own2 + RIM, source_col - own2, source_col)
    inside = (source_col >= RIM) & (source_col < own2 + RIM)
    hot_ref[:, 2 * own2 :] = one_hot(jnp.where(inside, -1.0, rim_col), 2 * RIM)
    length_wide = jnp.concatenate([column(mdist_ref[...])] * (width // LANES), axis=1)
    acc_ref[...] = length_wide * pvec_ref[1:2, :] + pvec_ref[0:1, :]

    for k in range(1, owners):
        sends[k - 1].wait_recv()
        forwards[k].start()
    loads[4].wait()
    loads[5].wait()
    for copy in forwards:
        copy.wait_recv()

    count = owners * CAP
    got = [got_ref[...].astype(F32), got2_ref[...].astype(F32)]
    top = [g[:, 0:CAP, :].reshape(count, half + LANES) for g in got]
    bottom = [g[:, CAP:, :].reshape(count, half + LANES) for g in got]
    top = jnp.concatenate(top, axis=0)
    bottom = jnp.concatenate(bottom, axis=0)
    mine = jnp.where(bottom[:, half:] == sub.astype(F32), top[:, half:], -1.0)
    hot = one_hot(mine, rows)
    pre = jnp.concatenate([top[:, :half], bottom[:, :half]], axis=1) + dot(hot, receiver_proj)
    hidden = silu(pre).astype(BF16)
    aggregate = lax.dot_general(
        hot, hidden, (((0,), (0,)), ((), ())), preferred_element_type=F32
    )
    hid_ref[0:rows, :] = aggregate.astype(BF16)

    own_at = RIM + sub * rows
    piece = RIM // PARTS
    rim_at = (1 - sub) * (RIM + own2)
    step = 2 * sub - 1
    target, source = me + step, me - step
    has_target = (target >= 0) & (target < owners)
    has_source = (source >= 0) & (source < owners)

    def update(start, size):
        at = pl.ds(pl.multiple_of(start, RIM), size)
        value = base_ref[at, :] + dot(hid_ref[at, :], wn_ref[1])
        node_hidden = silu(value).astype(BF16)
        fresh = mesh_ref[at, :].astype(F32) + dot(node_hidden, wo_ref[...])
        fresh = fresh.astype(BF16)
        enc_out[at, :] = fresh
        ext_ref[pl.ds(pl.multiple_of(own_at + start, RIM), size), :] = fresh

    def to_sibling(start, size, index):
        at = pl.ds(pl.multiple_of(own_at + start, RIM), size)
        return send(
            ext_ref.at[at], ext_ref.at[at], (sib_send.at[index], sib_recv.at[index]), sibling
        )

    edge_start, rest_start = sub * (rows - RIM), (1 - sub) * RIM
    update(edge_start, RIM)
    rims = []
    for i in range(PARTS):
        src = pl.ds(pl.multiple_of(own_at + edge_start + i * piece, piece), piece)
        dst = pl.ds(pl.multiple_of(rim_at + i * piece, piece), piece)
        rims.append(
            send(
                ext_ref.at[src],
                ext_ref.at[dst],
                (rim_send.at[i], rim_recv.at[i]),
                owner_id(lax.clamp(0, target, owners - 1)),
            )
        )

    @pl.when(has_target)
    def _():
        for copy in rims:
            copy.start()

    @pl.when(jnp.logical_not(has_source))
    def _():
        ext_ref[pl.ds(pl.multiple_of(rim_at, RIM), RIM), :] = jnp.zeros((RIM, width), BF16)

    shares = [to_sibling(edge_start, RIM, 0), to_sibling(rest_start, rows - RIM, 1)]
    shares[0].start()
    update(rest_start, rows - RIM)
    shares[1].start()

    def project(at, size):
        block = ext_ref[pl.ds(pl.multiple_of(at, RIM), size), :]
        to = pl.multiple_of(at - RIM, RIM)
        table_ref[pl.ds(to, size), :] = dot(block, wp_ref[0]).astype(BF16)
        table_ref[pl.ds(pl.multiple_of(to + own2, RIM), size), :] = dot(
            block, wp_ref[1]
        ).astype(BF16)

    project(own_at, rows)
    shares[0].wait_recv()
    shares[1].wait_recv()
    project(RIM + (1 - sub) * rows, rows)
    chunk = 512
    for at in range(0, edges, chunk):
        acc_ref[at : at + chunk, :] += dot(
            hot_ref[at : at + chunk, 0 : 2 * own2], table_ref[0 : 2 * own2, :]
        )

    passed = []
    for i in range(PARTS):
        at = pl.ds(pl.multiple_of(rim_at + i * piece, piece), piece)
        passed.append(
            send(ext_ref.at[at], ext_ref.at[at], (rfw_send.at[i], rfw_recv.at[i]), sibling)
        )
    for i in range(PARTS):

        @pl.when(has_source)
        def _():
            rims[i].wait_recv()

        passed[i].start()

    def project_rim(at, to):
        block = ext_ref[pl.ds(pl.multiple_of(at, RIM), RIM), :]
        table_ref[pl.ds(pl.multiple_of(2 * own2 + to, RIM), RIM), :] = dot(
            block, wp_ref[0]
        ).astype(BF16)

    project_rim(rim_at, (1 - sub) * RIM)
    for copy in passed:
        copy.wait_recv()
    project_rim(sub * (RIM + own2), sub * RIM)
    for at in range(0, edges, chunk):
        value = acc_ref[at : at + chunk, :] + dot(
            hot_ref[at : at + chunk, 2 * own2 :], table_ref[2 * own2 :, :]
        )
        hid_ref[at : at + chunk, :] = silu(value).astype(BF16)

    def summed(which):
        at = pl.ds(pl.multiple_of(which * rows, RIM), rows)
        return dot(hot_t_ref[at, :], hid_ref[...]).astype(BF16)

    part_ref[...] = summed(1 - sub)
    partial = send(part_ref, other_ref, (par_send.at[0], par_recv.at[0]), sibling)
    partial.start()
    mine = summed(sub).astype(F32)
    partial.wait_recv()
    agg_out[...] = (mine + other_ref[...].astype(F32)).astype(BF16)

    for copy in sends + forwards + shares + passed + [partial]:
        copy.wait_send()

    @pl.when(has_target)
    def _():
        for copy in rims:
            copy.wait_send()


def on_device(owners, feats, *args):
    grid_lat, mesh_lat = args[0], args[1]
    edges, slots = args[6].shape[1], args[2].shape[1]
    rows, width = mesh_lat.shape
    own2 = 2 * rows
    vmem = pl.BlockSpec(memory_space=pltpu.VMEM)
    smem = pl.BlockSpec(memory_space=pltpu.SMEM)
    hbm = pl.BlockSpec(memory_space=pl.ANY)
    in_specs = [hbm, hbm, vmem, vmem, smem, vmem, vmem, vmem, smem, vmem]
    in_specs += [hbm] * 4 + [vmem] * 2
    message = (owners, 2 * CAP, width // 2 + LANES)
    dma = pltpu.SemaphoreType.DMA
    scratch = [
        pltpu.VMEM(grid_lat.shape, BF16),
        pltpu.VMEM(mesh_lat.shape, BF16),
        pltpu.VMEM(args[10].shape, BF16),
        pltpu.VMEM(args[11].shape, BF16),
        pltpu.VMEM(args[12].shape, BF16),
        pltpu.VMEM(args[13].shape, BF16),
        pltpu.VMEM(message, BF16),
        pltpu.VMEM(message, BF16),
        pltpu.VMEM(message, BF16),
        pltpu.VMEM((rows, width), F32),
        pltpu.VMEM((edges, 2 * own2 + 2 * RIM), BF16),
        pltpu.VMEM((own2, edges), BF16),
        pltpu.VMEM((own2 + 2 * RIM, width), BF16),
        pltpu.VMEM((2 * own2 + 2 * RIM, width), BF16),
        pltpu.VMEM((edges, width), F32),
        pltpu.VMEM((edges, width), BF16),
        pltpu.VMEM((rows, width), BF16),
        pltpu.VMEM((rows, width), BF16),
        dma((6,)),
        dma((owners,)),
        dma((owners,)),
        dma((owners,)),
        dma((owners,)),
        dma((2,)),
        dma((2,)),
        dma((PARTS,)),
        dma((PARTS,)),
        dma((PARTS,)),
        dma((PARTS,)),
        dma((1,)),
        dma((1,)),
    ]
    return pl.pallas_call(
        functools.partial(kernel, owners, feats),
        out_shape=[jax.ShapeDtypeStruct((rows, width), BF16)] * 2,
        in_specs=in_specs,
        out_specs=[vmem, vmem],
        scratch_shapes=scratch,
        compiler_params=pltpu.CompilerParams(
            collective_id=0, has_side_effects=True, vmem_limit_bytes=40 * 1024 * 1024
        ),
    )(*args)


def solution(mesh):
    split = P(("groups", "dom", "feat", "sub"), None)
    feats = mesh.shape["feat"]
    owners = mesh.shape["dom"] * feats
    return jax.shard_map(
        functools.partial(on_device, owners, feats),
        mesh=mesh,
        in_specs=(split,) * 10 + (P(),) * 6,
        out_specs=(split, split),
        check_vma=False,
    )
```

time: 103 us -> 33.4 us (0.32)
  waiting for transfers between devices: 26.2 us -> 0 us
  starting transfers between devices: 21.6 us -> 0 us
  Pallas kernels: 0 us -> 19.2 us
  matrix products: 15.1 us -> 0 us
  between operations: 15 us -> 1.38 us
  other arithmetic: 6.61 us -> 0 us
  blocking collectives: 4.57 us -> 0 us
  local copies, waits for them, and re-layouts: 13.4 us -> 12.2 us
    pallas_call x0 -> x1, Pallas kernels: none -> 19.2 us  [on_device(): pl.pallas_call(functools.partial(kernel, owners, feats), out_shape=[jax.S...]
    all_to_all x3 -> x0, starting transfers between devices: 16.6 us -> none  [the longest x1 7.25 us: on_device(): lax.all_to_all(slot_lengths, ('dom', 'feat'), split_axis=0, concat_axis=0...]
    dot_general x8 -> x0, matrix products: 15.1 us -> none  [the longest x2 6.93 us: edge_aggregate(): jnp.dot(incidence, hidden_edge, preferred_element_type=jnp.float32)]
    reduce_scatter x2 -> x0, waiting for transfers between devices: 14.6 us -> none  [edge_aggregate(): lax.psum_scatter(partial_value.astype(jnp.bfloat16), 'sub', scatter_dimen...]
    all_to_all x3 -> x0, waiting for transfers between devices: 11.7 us -> none  [the longest x1 6.29 us: on_device(): lax.all_to_all(slot_tags, ('dom', 'feat'), split_axis=0, concat_axis=0, t...]
    gather x4 -> x0, local copies, waits for them, and re-layouts: 11.3 us -> none  [the longest x2 5.61 us: edge_aggregate(): pre_act = source_terms + jnp.take(receiver_proj, receiver, axis=0)]
    unnamed x22 -> x32, local copies, waits for them, and re-layouts: 1.08 us -> 12.2 us
    ppermute x2 -> x0, starting transfers between devices: 4.9 us -> none  [the longest x1 3.61 us: extended_2(): before = lax.ppermute(last, axis, up)]
  transfers between devices with their start and end apart: 7 -> 0, of which waited for: 4 -> 0; matrix products, arithmetic and copies ran while one was open for 17% -> 0% of each run, Pallas kernels for 0% -> 0%
where the time goes in v1:
time: 33.4 us; the launch traced here: 32.8 us
  Pallas kernels  19.2 us (57%)
  local copies, waits for them, and re-layouts  12.2 us (37%)
  between operations  1.38 us (4%)
    pallas_call x1, Pallas kernels, on_device(): pl.pallas_call(functools.partial(kernel, owners, feats), out_shape=[jax.S...  19.2 us
    unnamed x32, local copies, waits for them, and re-layouts  12.2 us

profile of v1, /device:TPU:0, one launch (start us, length us, event | category | flops | bytes accessed | tf_op | source)
XLA Modules:
  0.0 32.8 jit_solution(10891222828963203279)
XLA Ops:
  0.6 0.0 copy-start.13
  0.6 0.0 copy-start.12
  0.7 0.0 copy-start.11
  1.3 0.0 copy-done.13
  1.3 0.0 copy-done.12
  1.4 0.0 copy-done.11
  1.4 0.0 copy-start
  1.4 1.2 %copy-done = bf16[2,512,512]{2,1,0:T(8,128)(2,1)S(1)} copy-done((bf16[2,512,512]{2,1,0:T(8,128)(2,1)S(1)}, bf16[2,512,512]{2,1,0:T(8,128)(2,1)}, u32[]{:S(2)}) %copy-start) | copy-done | bytes 1048600
  2.6 0.0 copy-start.1
  2.6 1.2 %copy-done.1 = bf16[2,512,512]{2,1,0:T(8,128)(2,1)S(1)} copy-done((bf16[2,512,512]{2,1,0:T(8,128)(2,1)S(1)}, bf16[2,512,512]{2,1,0:T(8,128)(2,1)}, u32[]{:S(2)}) %copy-start.1) | copy-done | bytes 1048600
  3.8 0.0 copy-start.2
  3.8 1.2 %copy-done.2 = bf16[2,512,512]{2,1,0:T(8,128)(2,1)S(1)} copy-done((bf16[2,512,512]{2,1,0:T(8,128)(2,1)S(1)}, bf16[2,512,512]{2,1,0:T(8,128)(2,1)}, u32[]{:S(2)}) %copy-start.2) | copy-done | bytes 1048600
  5.0 0.0 copy-start.3
  5.0 1.0 %copy-done.3 = bf16[512,512]{1,0:T(8,128)(2,1)S(1)} copy-done((bf16[512,512]{1,0:T(8,128)(2,1)S(1)}, bf16[512,512]{1,0:T(8,128)(2,1)}, u32[]{:S(2)}) %copy-start.3) | copy-done | bytes 524312
  6.1 0.0 copy-start.4
  6.1 1.0 %copy-done.4 = bf16[512,512]{1,0:T(8,128)(2,1)S(1)} copy-done((bf16[512,512]{1,0:T(8,128)(2,1)S(1)}, bf16[512,512]{1,0:T(8,128)(2,1)}, u32[]{:S(2)}) %copy-start.4) | copy-done | bytes 524312
  7.1 0.0 copy-start.5
  7.1 0.9 %copy-done.5 = bf16[256,512]{1,0:T(8,128)(2,1)S(1)} copy-done((bf16[256,512]{1,0:T(8,128)(2,1)S(1)}, bf16[256,512]{1,0:T(8,128)(2,1)}, u32[]{:S(2)}) %copy-start.5) | copy-done | bytes 262168
  8.1 0.0 copy-start.6
  8.1 0.7 %copy-done.6 = f32[3,512]{1,0:T(4,128)S(1)} copy-done((f32[3,512]{1,0:T(4,128)S(1)}, f32[3,512]{1,0:T(4,128)}, u32[]{:S(2)}) %copy-start.6) | copy-done | bytes 6168
  8.8 0.0 copy-start.7
  8.8 0.7 %copy-done.7 = s32[1,1536]{1,0:T(1,128)S(1)} copy-done((s32[1,1536]{1,0:T(1,128)S(1)}, s32[1,1536]{1,0:T(1,128)}, u32[]{:S(2)}) %copy-start.7) | copy-done | bytes 6168
  9.5 0.0 copy-start.8
  9.5 0.7 %copy-done.8 = s32[1,1536]{1,0:T(1,128)S(1)} copy-done((s32[1,1536]{1,0:T(1,128)S(1)}, s32[1,1536]{1,0:T(1,128)}, u32[]{:S(2)}) %copy-start.8) | copy-done | bytes 6168
  10.2 0.0 copy-start.9
  10.2 0.7 %copy-done.9 = f32[1,1536]{1,0:T(1,128)S(1)} copy-done((f32[1,1536]{1,0:T(1,128)S(1)}, f32[1,1536]{1,0:T(1,128)}, u32[]{:S(2)}) %copy-start.9) | copy-done | bytes 6168
  10.9 0.0 copy-start.10
  10.9 0.7 %copy-done.10 = f32[2,512]{1,0:T(2,128)S(1)} copy-done((f32[2,512]{1,0:T(2,128)S(1)}, f32[2,512]{1,0:T(2,128)}, u32[]{:S(2)}) %copy-start.10) | copy-done | bytes 4120
  11.5 0.0 copy-start.14
  11.5 0.7 %copy-done.14 = bf16[1,64]{1,0:T(2,128)(2,1)S(1)} copy-done((bf16[1,64]{1,0:T(2,128)(2,1)S(1)}, bf16[1,64]{1,0:T(2,128)(2,1)}, u32[]{:S(2)}) %copy-start.14) | copy-done | bytes 152
  12.2 19.2 %shard_map.167 = (bf16[256,512]{1,0:T(8,128)(2,1)S(1)}, bf16[256,512]{1,0:T(8,128)(2,1)S(1)}) custom-call(bf16[512,512]{1,0:T(8,128)(2,1)S(1)} %copy-done.3, bf16[256,512]{1,0:T(8,128)(2,1)S(1)} %copy-done.5, s32[1,64]{1,0:T(1,128)S(1)} %copy-done.11, s32[1,64]{1,0:T(1,128)S(1)} %copy-done.12, s32[1,8]{1,0:T(1,128)S(1)} %copy-done.13, ...), custom_call_target="tpu_custom_call" | custom-call | tf_op jit(solution)/shard_map/pallas_call | solution.py:387
  31.4 0.7 %copy.21 = bf16[256,512]{1,0:T(8,128)(2,1)} copy(bf16[256,512]{1,0:T(8,128)(2,1)S(1)} %get-tuple-element.4) | data formatting | bytes 524288
  32.1 0.7 %copy.22 = bf16[256,512]{1,0:T(8,128)(2,1)} copy(bf16[256,512]{1,0:T(8,128)(2,1)S(1)} %get-tuple-element.5) | data formatting | bytes 524288
Async XLA Ops:
  0.6 0.7 %copy-start.13 = (s32[1,8]{1,0:T(1,128)S(1)}, s32[1,8]{1,0:T(1,128)}, u32[]{:S(2)}) copy-start(s32[1,8]{1,0:T(1,128)} %gcount_ref.1) | copy-start | bytes 100
  0.6 0.7 %copy-start.12 = (s32[1,64]{1,0:T(1,128)S(1)}, s32[1,64]{1,0:T(1,128)}, u32[]{:S(2)}) copy-start(s32[1,64]{1,0:T(1,128)} %gdst_ref.1) | copy-start | bytes 772
  0.7 0.7 %copy-start.11 = (s32[1,64]{1,0:T(1,128)S(1)}, s32[1,64]{1,0:T(1,128)}, u32[]{:S(2)}) copy-start(s32[1,64]{1,0:T(1,128)} %gsrc_ref.1) | copy-start | bytes 772
  1.4 1.2 %copy-start = (bf16[2,512,512]{2,1,0:T(8,128)(2,1)S(1)}, bf16[2,512,512]{2,1,0:T(8,128)(2,1)}, u32[]{:S(2)}) copy-start(bf16[2,512,512]{2,1,0:T(8,128)(2,1)} %we_hbm.1) | copy-start | bytes 3145732
  2.6 1.2 %copy-start.1 = (bf16[2,512,512]{2,1,0:T(8,128)(2,1)S(1)}, bf16[2,512,512]{2,1,0:T(8,128)(2,1)}, u32[]{:S(2)}) copy-start(bf16[2,512,512]{2,1,0:T(8,128)(2,1)} %wn_hbm.1) | copy-start | bytes 3145732
  3.8 1.2 %copy-start.2 = (bf16[2,512,512]{2,1,0:T(8,128)(2,1)S(1)}, bf16[2,512,512]{2,1,0:T(8,128)(2,1)}, u32[]{:S(2)}) copy-start(bf16[2,512,512]{2,1,0:T(8,128)(2,1)} %wp_hbm.1) | copy-start | bytes 3145732
  5.0 1.0 %copy-start.3 = (bf16[512,512]{1,0:T(8,128)(2,1)S(1)}, bf16[512,512]{1,0:T(8,128)(2,1)}, u32[]{:S(2)}) copy-start(bf16[512,512]{1,0:T(8,128)(2,1)} %grid_hbm.1) | copy-start | bytes 1572868
  6.1 1.0 %copy-start.4 = (bf16[512,512]{1,0:T(8,128)(2,1)S(1)}, bf16[512,512]{1,0:T(8,128)(2,1)}, u32[]{:S(2)}) copy-start(bf16[512,512]{1,0:T(8,128)(2,1)} %wo_hbm.1) | copy-start | bytes 1572868
  7.1 0.9 %copy-start.5 = (bf16[256,512]{1,0:T(8,128)(2,1)S(1)}, bf16[256,512]{1,0:T(8,128)(2,1)}, u32[]{:S(2)}) copy-start(bf16[256,512]{1,0:T(8,128)(2,1)} %mesh_hbm.1) | copy-start | bytes 786436
  8.1 0.7 %copy-start.6 = (f32[3,512]{1,0:T(4,128)S(1)}, f32[3,512]{1,0:T(4,128)}, u32[]{:S(2)}) copy-start(f32[3,512]{1,0:T(4,128)} %evec_ref.1) | copy-start | bytes 18436
  8.8 0.7 %copy-start.7 = (s32[1,1536]{1,0:T(1,128)S(1)}, s32[1,1536]{1,0:T(1,128)}, u32[]{:S(2)}) copy-start(s32[1,1536]{1,0:T(1,128)} %msrc_ref.1) | copy-start | bytes 18436
  9.5 0.7 %copy-start.8 = (s32[1,1536]{1,0:T(1,128)S(1)}, s32[1,1536]{1,0:T(1,128)}, u32[]{:S(2)}) copy-start(s32[1,1536]{1,0:T(1,128)} %mdst_ref.1) | copy-start | bytes 18436
  10.2 0.7 %copy-start.9 = (f32[1,1536]{1,0:T(1,128)S(1)}, f32[1,1536]{1,0:T(1,128)}, u32[]{:S(2)}) copy-start(f32[1,1536]{1,0:T(1,128)} %mdist_ref.1) | copy-start | bytes 18436
  10.9 0.7 %copy-start.10 = (f32[2,512]{1,0:T(2,128)S(1)}, f32[2,512]{1,0:T(2,128)}, u32[]{:S(2)}) copy-start(f32[2,512]{1,0:T(2,128)} %pvec_ref.1) | copy-start | bytes 12292
  11.5 0.7 %copy-start.14 = (bf16[1,64]{1,0:T(2,128)(2,1)S(1)}, bf16[1,64]{1,0:T(2,128)(2,1)}, u32[]{:S(2)}) copy-start(bf16[1,64]{1,0:T(2,128)(2,1)} %gdist_ref.1) | copy-start | bytes 388

commit v2 on v1

--- a/solution.py
+++ b/solution.py
@@ -11,6 +11,7 @@
 RIM = 128
 LANES = 128
 PARTS = 2
+LIMIT = 63 * 1024 * 1024
 MESH = pl.DeviceIdType.MESH
 BF16 = jnp.bfloat16
 F32 = jnp.float32
@@ -47,6 +48,22 @@
     feats,
     grid_hbm,
     mesh_hbm,
+    gsrc_hbm,
+    gdst_hbm,
+    gcount_hbm,
+    gdist_hbm,
+    msrc_hbm,
+    mdst_hbm,
+    mcount_hbm,
+    mdist_hbm,
+    we_hbm,
+    wn_hbm,
+    wo_hbm,
+    wp_hbm,
+    evec_hbm,
+    pvec_hbm,
+    enc_out,
+    agg_out,
     gsrc_ref,
     gdst_ref,
     gcount_ref,
@@ -55,14 +72,8 @@
     mdst_ref,
     mcount_ref,
     mdist_ref,
-    we_hbm,
-    wn_hbm,
-    wo_hbm,
-    wp_hbm,
     evec_ref,
     pvec_ref,
-    enc_out,
-    agg_out,
     grid_ref,
     mesh_ref,
     we_ref,
@@ -81,6 +92,8 @@
     hid_ref,
     part_ref,
     other_ref,
+    enc_ref,
+    agg_ref,
     load_sem,
     a2a_send,
     a2a_recv,
@@ -124,34 +137,54 @@
         )
 
     pairs = (
+        (gsrc_hbm, gsrc_ref),
         (grid_hbm, grid_ref),
-        (we_hbm, we_ref),
+        (we_hbm.at[0], we_ref.at[0]),
+        (gdst_hbm, gdst_ref),
+        (gcount_hbm, gcount_ref),
+        (gdist_hbm, gdist_ref),
+        (evec_hbm, evec_ref),
         (mesh_hbm, mesh_ref),
+        (we_hbm.at[1], we_ref.at[1]),
         (wn_hbm, wn_ref),
+        (msrc_hbm, msrc_ref),
+        (mdst_hbm, mdst_ref),
+        (mcount_hbm, mcount_ref),
+        (mdist_hbm, mdist_ref),
+        (pvec_hbm, pvec_ref),
         (wo_hbm, wo_ref),
         (wp_hbm, wp_ref),
     )
     loads = [
         pltpu.make_async_copy(src, dst, load_sem.at[i]) for i, (src, dst) in enumerate(pairs)
     ]
-    for load in loads:
+    for load in loads[:7]:
         load.start()
+
+    def loaded(first, last):
+        for load in loads[first : last + 1]:
+            load.wait()
+
+    loaded(0, 0)
+    source_hot = one_hot(column(gsrc_ref[...]), grid_ref.shape[0])
+    loaded(1, 1)
+    picked = dot(source_hot, grid_ref[...]).astype(BF16)
+    loaded(2, 2)
+    for load in loads[7:]:
+        load.start()
+    term = dot(picked, we_ref[0])
+    loaded(3, 6)
 
     gdst = gdst_ref[...]
     upper = (gdst >= rows).astype(jnp.int32)
     upper_col = column(upper)
     lower_col = column(gdst - rows * upper)
     length_col = column(gdist_ref[...])
-    source_hot = one_hot(column(gsrc_ref[...]), grid_ref.shape[0])
     slot = lax.broadcasted_iota(jnp.int32, (CAP, LANES), 0)
     live = jnp.concatenate(
         [jnp.where(slot < gcount_ref[0, o], 1.0, 0.0) for o in range(owners)], axis=0
     )
     lower_col = jnp.where(live > 0.5, lower_col, -1.0)
-    loads[0].wait()
-    picked = dot(source_hot, grid_ref[...]).astype(BF16)
-    loads[1].wait()
-    term = dot(picked, we_ref[0])
     term = term + jnp.concatenate([length_col] * (width // LANES), axis=1) * evec_ref[1:2, :]
     term = term + evec_ref[0:1, :]
     top = jnp.concatenate([term[:, :half], lower_col], axis=1)
@@ -179,10 +212,11 @@
     got_ref[0] = msg_ref[me]
     forwards[0].start()
 
-    loads[2].wait()
+    loaded(7, 8)
     receiver_proj = dot(mesh_ref[...], we_ref[1]).astype(BF16)
-    loads[3].wait()
+    loaded(9, 9)
     base_ref[...] = dot(mesh_ref[...], wn_ref[0]) + evec_ref[2:3, :]
+    loaded(10, 14)
     edge = lax.broadcasted_iota(jnp.int32, (1, edges), 1)
     tags = jnp.where(edge < mcount_ref[0, 0], mdst_ref[...], -1)
     node = lax.broadcasted_iota(jnp.int32, (own2, edges), 0)
@@ -199,8 +233,7 @@
     for k in range(1, owners):
         sends[k - 1].wait_recv()
         forwards[k].start()
-    loads[4].wait()
-    loads[5].wait()
+    loaded(15, 16)
     for copy in forwards:
         copy.wait_recv()
 
@@ -233,7 +266,7 @@
         node_hidden = silu(value).astype(BF16)
         fresh = mesh_ref[at, :].astype(F32) + dot(node_hidden, wo_ref[...])
         fresh = fresh.astype(BF16)
-        enc_out[at, :] = fresh
+        enc_ref[at, :] = fresh
         ext_ref[pl.ds(pl.multiple_of(own_at + start, RIM), size), :] = fresh
 
     def to_sibling(start, size, index):
@@ -270,6 +303,8 @@
     shares[0].start()
     update(rest_start, rows - RIM)
     shares[1].start()
+    enc_store = pltpu.make_async_copy(enc_ref, enc_out, load_sem.at[0])
+    enc_store.start()
 
     def project(at, size):
         block = ext_ref[pl.ds(pl.multiple_of(at, RIM), size), :]
@@ -328,7 +363,9 @@
     partial.start()
     mine = summed(sub).astype(F32)
     partial.wait_recv()
-    agg_out[...] = (mine + other_ref[...].astype(F32)).astype(BF16)
+    agg_ref[...] = (mine + other_ref[...].astype(F32)).astype(BF16)
+    agg_store = pltpu.make_async_copy(agg_ref, agg_out, load_sem.at[1])
+    agg_store.start()
 
     for copy in sends + forwards + shares + passed + [partial]:
         copy.wait_send()
@@ -337,6 +374,27 @@
     def _():
         for copy in rims:
             copy.wait_send()
+
+    enc_store.wait()
+    agg_store.wait()
+
+
+def finish(enc_in, agg_in, enc_out, agg_out, enc_ref, agg_ref, sems):
+    reads = [
+        pltpu.make_async_copy(enc_in, enc_ref, sems.at[0]),
+        pltpu.make_async_copy(agg_in, agg_ref, sems.at[1]),
+    ]
+    writes = [
+        pltpu.make_async_copy(enc_ref, enc_out, sems.at[2]),
+        pltpu.make_async_copy(agg_ref, agg_out, sems.at[3]),
+    ]
+    for copy in reads:
+        copy.start()
+    for read, write in zip(reads, writes):
+        read.wait()
+        write.start()
+    for copy in writes:
+        copy.wait()
 
 
 def on_device(owners, feats, *args):
@@ -344,14 +402,15 @@
     edges, slots = args[6].shape[1], args[2].shape[1]
     rows, width = mesh_lat.shape
     own2 = 2 * rows
-    vmem = pl.BlockSpec(memory_space=pltpu.VMEM)
-    smem = pl.BlockSpec(memory_space=pltpu.SMEM)
-    hbm = pl.BlockSpec(memory_space=pl.ANY)
-    in_specs = [hbm, hbm, vmem, vmem, smem, vmem, vmem, vmem, smem, vmem]
-    in_specs += [hbm] * 4 + [vmem] * 2
+    hbm = pl.BlockSpec(memory_space=pltpu.HBM)
     message = (owners, 2 * CAP, width // 2 + LANES)
     dma = pltpu.SemaphoreType.DMA
+    small = [args[i] for i in (2, 3, 4, 5, 6, 7, 8, 9, 14, 15)]
     scratch = [
+        (pltpu.SMEM if i in (2, 6) else pltpu.VMEM)(a.shape, a.dtype)
+        for i, a in enumerate(small)
+    ]
+    scratch += [
         pltpu.VMEM(grid_lat.shape, BF16),
         pltpu.VMEM(mesh_lat.shape, BF16),
         pltpu.VMEM(args[10].shape, BF16),
@@ -370,7 +429,9 @@
         pltpu.VMEM((edges, width), BF16),
         pltpu.VMEM((rows, width), BF16),
         pltpu.VMEM((rows, width), BF16),
-        dma((6,)),
+        pltpu.VMEM((rows, width), BF16),
+        pltpu.VMEM((rows, width), BF16),
+        dma((17,)),
         dma((owners,)),
         dma((owners,)),
         dma((owners,)),
@@ -384,16 +445,24 @@
         dma((1,)),
         dma((1,)),
     ]
-    return pl.pallas_call(
+    shapes = [jax.ShapeDtypeStruct((rows, width), BF16)] * 2
+    outs = pl.pallas_call(
         functools.partial(kernel, owners, feats),
-        out_shape=[jax.ShapeDtypeStruct((rows, width), BF16)] * 2,
-        in_specs=in_specs,
-        out_specs=[vmem, vmem],
+        out_shape=shapes,
+        in_specs=[hbm] * 16,
+        out_specs=[hbm, hbm],
         scratch_shapes=scratch,
         compiler_params=pltpu.CompilerParams(
-            collective_id=0, has_side_effects=True, vmem_limit_bytes=40 * 1024 * 1024
+            collective_id=0, has_side_effects=True, vmem_limit_bytes=LIMIT
         ),
     )(*args)
+    return pl.pallas_call(
+        finish,
+        out_shape=shapes,
+        in_specs=[hbm, hbm],
+        out_specs=[hbm, hbm],
+        scratch_shapes=[pltpu.VMEM((rows, width), BF16)] * 2 + [dma((4,))],
+    )(*outs)
 
 
 def solution(mesh):

time: 33.4 us -> 23.2 us (0.69); the launches traced: 32.8 us -> 23 us
  local copies, waits for them, and re-layouts: 12.2 us -> 0 us
  Pallas kernels: 19.2 us -> 21.7 us
    unnamed x32 -> x0, local copies, waits for them, and re-layouts: 12.2 us -> none
    pallas_call x1 -> x2, Pallas kernels: 19.2 us -> 21.7 us  [the longest x1 20 us: on_device(): pl.pallas_call(functools.partial(kernel, owners, feats), out_shape=shapes...]
where the time goes in v2:
time: 23.2 us; the launch traced here: 23 us
  Pallas kernels  21.7 us (94%)
  between operations  1.29 us (6%)
    pallas_call x1, Pallas kernels, on_device(): pl.pallas_call(functools.partial(kernel, owners, feats), out_shape=shapes...  20 us
    pallas_call x1, Pallas kernels, on_device(): pl.pallas_call(finish, out_shape=shapes, in_specs=[hbm, hbm], out_specs=[...  1.77 us

profile of v2, /device:TPU:0, one launch (start us, length us, event | category | flops | bytes accessed | tf_op | source)
XLA Modules:
  0.0 23.0 jit_solution(5577361534491494716)
XLA Ops:
  1.3 20.0 %shard_map.167 = (bf16[256,512]{1,0:T(8,128)(2,1)}, bf16[256,512]{1,0:T(8,128)(2,1)}) custom-call(bf16[512,512]{1,0:T(8,128)(2,1)} %grid_hbm.1, bf16[256,512]{1,0:T(8,128)(2,1)} %mesh_hbm.1, s32[1,64]{1,0:T(1,128)} %gsrc_hbm.1, s32[1,64]{1,0:T(1,128)} %gdst_hbm.1, s32[1,8]{1,0:T(1,128)} %gcount_hbm.1, bf16[1,64]{1,0:T(2,128)(2,1)} %gdist_hbm.1, ...), custom_call_target="tpu_custom_call" | custom-call | tf_op jit(solution)/shard_map/pallas_call | solution.py:449
  21.3 1.8 %shard_map.168 = (bf16[256,512]{1,0:T(8,128)(2,1)}, bf16[256,512]{1,0:T(8,128)(2,1)}) custom-call(bf16[256,512]{1,0:T(8,128)(2,1)} %get-tuple-element.4.enc_in, bf16[256,512]{1,0:T(8,128)(2,1)} %get-tuple-element.5.agg_in), custom_call_target="tpu_custom_call" | custom-call | tf_op jit(solution)/shard_map/pallas_call | solution.py:459

commit v3 on v2

--- a/solution.py
+++ b/solution.py
@@ -318,25 +318,25 @@
     shares[0].wait_recv()
     shares[1].wait_recv()
     project(RIM + (1 - sub) * rows, rows)
-    chunk = 512
-    for at in range(0, edges, chunk):
-        acc_ref[at : at + chunk, :] += dot(
-            hot_ref[at : at + chunk, 0 : 2 * own2], table_ref[0 : 2 * own2, :]
-        )
-
     passed = []
     for i in range(PARTS):
         at = pl.ds(pl.multiple_of(rim_at + i * piece, piece), piece)
         passed.append(
             send(ext_ref.at[at], ext_ref.at[at], (rfw_send.at[i], rfw_recv.at[i]), sibling)
         )
-    for i in range(PARTS):
-
-        @pl.when(has_source)
-        def _():
-            rims[i].wait_recv()
-
-        passed[i].start()
+    chunk = 512
+    for at in range(0, edges, chunk):
+        acc_ref[at : at + chunk, :] += dot(
+            hot_ref[at : at + chunk, 0 : 2 * own2], table_ref[0 : 2 * own2, :]
+        )
+        if at == 0:
+            for i in range(PARTS):
+
+                @pl.when(has_source)
+                def _():
+                    rims[i].wait_recv()
+
+                passed[i].start()
 
     def project_rim(at, to):
         block = ext_ref[pl.ds(pl.multiple_of(at, RIM), RIM), :]

time: 23.2 us -> 22.8 us (0.983)
  the two profiles are of different devices: /device:TPU:0 before, /device:TPU:29 now
where the time goes in v3:
time: 22.8 us; the launch traced here: 22.6 us
  Pallas kernels  21.4 us (94%)
  between operations  1.29 us (6%)
    pallas_call x1, Pallas kernels, on_device(): pl.pallas_call(functools.partial(kernel, owners, feats), out_shape=shapes...  19.6 us
    pallas_call x1, Pallas kernels, on_device(): pl.pallas_call(finish, out_shape=shapes, in_specs=[hbm, hbm], out_specs=[...  1.77 us

profile of v3, /device:TPU:29, one launch (start us, length us, event | category | flops | bytes accessed | tf_op | source)
XLA Modules:
  0.0 22.6 jit_solution(1309886046030881904)
XLA Ops:
  1.3 19.6 %shard_map.167 = (bf16[256,512]{1,0:T(8,128)(2,1)}, bf16[256,512]{1,0:T(8,128)(2,1)}) custom-call(bf16[512,512]{1,0:T(8,128)(2,1)} %grid_hbm.1, bf16[256,512]{1,0:T(8,128)(2,1)} %mesh_hbm.1, s32[1,64]{1,0:T(1,128)} %gsrc_hbm.1, s32[1,64]{1,0:T(1,128)} %gdst_hbm.1, s32[1,8]{1,0:T(1,128)} %gcount_hbm.1, bf16[1,64]{1,0:T(2,128)(2,1)} %gdist_hbm.1, ...), custom_call_target="tpu_custom_call" | custom-call | tf_op jit(solution)/shard_map/pallas_call | solution.py:449
  20.9 1.8 %shard_map.168 = (bf16[256,512]{1,0:T(8,128)(2,1)}, bf16[256,512]{1,0:T(8,128)(2,1)}) custom-call(bf16[256,512]{1,0:T(8,128)(2,1)} %get-tuple-element.4.enc_in, bf16[256,512]{1,0:T(8,128)(2,1)} %get-tuple-element.5.agg_in), custom_call_target="tpu_custom_call" | custom-call | tf_op jit(solution)/shard_map/pallas_call | solution.py:459
